TPU v7x, 128 devices: a whole 4x4x4 slice. The times are simulated.
128 devices in a mesh: obj: 8 (over y, core), scan: 16 (over z, x).
Axes of the slice: x: 4, y: 4, z: 4, core: 2. Of those that a mesh axis runs over, the one named last changes fastest.
Arguments:
- object_field: float32 [2, 4096, 8192], P(None, 'obj', 'scan'), may hold values from -6 to 6
- probe: float32 [2, 256, 256], replicated, may hold values from -3 to 3
- amplitudes: bfloat16 [8, 512, 256, 256], P('obj', 'scan'), may hold values from 0.25 to 2
- corner_row: int32 [8, 256, 2], P('obj', 'scan'), may hold values from -1 to 511, as said below
- corner_col: int32 [8, 256, 2], P('obj', 'scan'), may hold values from -1 to 511, as said below
Outputs:
- object_grad: float32 [2, 4096, 8192], P(None, 'obj', 'scan')
- probe_grad: float32 [16, 2, 256, 256], P('scan')
Inputs may be any that keep to these rules, and one draw needn't show every extreme that they name: A slot is live exactly when both corner_row and corner_col are 0 or more; the live slots of each (band, home tile, owner) list come first. In every band some owner has all 2 slots live from every home tile, and some slot is empty. A live position's window lies inside the object. `corner_col`: empty exactly where corner_row is empty.
All inputs are finite; a program needn't handle non-finite values.
Results may differ from a plain program's by a relative error of at most 0.011.
Values may be sent and summed in bfloat16 or wider, within the bound.
A program may use at most 128 MiB of HBM per device.

v0:
```python
import math

import jax
import jax.numpy as jnp
from jax import lax
from jax.sharding import PartitionSpec as P


def passed_along(shard, axis, by):
    size = lax.axis_size(axis)
    pairs = [(i, i + by) for i in range(size) if 0 <= i + by < size]
    return lax.ppermute(shard, axis, pairs)


def dft_tables(length, direction):
    grid_index = jnp.arange(length, dtype=jnp.int32)
    product = grid_index[:, None] * grid_index[None, :] % length
    phase_angle = 2.0 * math.pi / length * product.astype(jnp.float32)
    norm_scale = 1.0 / math.sqrt(length)
    cos_part = jnp.cos(phase_angle) * norm_scale
    sin_part = direction * jnp.sin(phase_angle) * norm_scale
    left_table = jnp.stack(
        [jnp.stack([cos_part, -sin_part], 1), jnp.stack([sin_part, cos_part], 1)], 0
    )
    right_table = jnp.stack(
        [jnp.stack([cos_part, sin_part], 1), jnp.stack([-sin_part, cos_part], 1)], 0
    )
    return (left_table.astype(jnp.bfloat16), right_table.astype(jnp.bfloat16))


def slot_block(patches, amplitude, probe, tables):
    fwd_left, fwd_right, inv_left, inv_right = tables
    field = patches.astype(jnp.float32)
    exit_wave = jnp.stack(
        [
            probe[0] * field[:, 0] - probe[1] * field[:, 1],
            probe[0] * field[:, 1] + probe[1] * field[:, 0],
        ],
        1,
    ).astype(jnp.bfloat16)
    half_done = jnp.einsum(
        "cuax,saxy->scuy", fwd_left, exit_wave, preferred_element_type=jnp.float32
    ).astype(jnp.bfloat16)
    far_field = jnp.einsum(
        "sauy,aycv->scuv", half_done, fwd_right, preferred_element_type=jnp.float32
    )
    magnitude = jnp.sqrt(far_field[:, 0] * far_field[:, 0] + far_field[:, 1] * far_field[:, 1])
    scale_factor = amplitude.astype(jnp.float32) / jnp.maximum(magnitude, 0.1) - 1.0
    difference = (far_field * scale_factor[:, None]).astype(jnp.bfloat16)
    back_half = jnp.einsum(
        "cuax,saxy->scuy", inv_left, difference, preferred_element_type=jnp.float32
    ).astype(jnp.bfloat16)
    near_field = jnp.einsum(
        "sauy,aycv->scuv", back_half, inv_right, preferred_element_type=jnp.float32
    )
    object_term = jnp.stack(
        [
            probe[0] * near_field[:, 0] + probe[1] * near_field[:, 1],
            probe[0] * near_field[:, 1] - probe[1] * near_field[:, 0],
        ],
        1,
    ).astype(jnp.bfloat16)
    probe_term = jnp.stack(
        [
            field[:, 0] * near_field[:, 0] + field[:, 1] * near_field[:, 1],
            field[:, 0] * near_field[:, 1] - field[:, 1] * near_field[:, 0],
        ],
        1,
    )
    return (object_term, jnp.sum(probe_term, 0))


def owner_work(arrived, measured, probe, tables):

    def compute(block_pair):
        return slot_block(block_pair[0], block_pair[1], probe, tables)

    def step_one(carry_unused, inputs):
        object_term, probe_term = compute(inputs)
        return (carry_unused, (object_term, probe_term))

    carry_unused, outputs = lax.scan(step_one, jnp.zeros((), jnp.float32), (arrived, measured))
    return outputs


def on_device(object_field, probe, amplitudes, corner_row, corner_col):
    patch_size = probe.shape[1]
    rows_tile = object_field.shape[1]
    cols_tile = object_field.shape[2]
    peer_count = lax.axis_size("scan")
    band_count = lax.axis_size("obj")
    capacity = corner_row.shape[2]
    tables = dft_tables(patch_size, -1.0) + dft_tables(patch_size, 1.0)
    anchor = jnp.zeros((), jnp.int32)
    rounded = object_field.astype(jnp.bfloat16)
    column_strip = passed_along(rounded[:, :, :patch_size], "scan", -1)
    widened = jnp.concatenate([rounded, column_strip], 2)
    lower_band = passed_along(widened[:, :patch_size, :], "obj", -1)
    extended = jnp.concatenate([widened, lower_band], 1)
    flat_rows = corner_row.reshape(-1)
    flat_cols = corner_col.reshape(-1)
    row_starts = jnp.maximum(flat_rows, 0)
    col_starts = jnp.maximum(flat_cols, 0)
    live_mask = flat_rows >= 0

    def cut_patch(row_start, col_start, keep_flag):
        window_cut = lax.dynamic_slice(
            extended, (anchor, row_start, col_start), (2, patch_size, patch_size)
        )
        return jnp.where(keep_flag, window_cut, jnp.zeros_like(window_cut))

    sending = jax.vmap(cut_patch)(row_starts, col_starts, live_mask)
    sending = sending.reshape(peer_count, capacity, 2, patch_size, patch_size)
    measured = amplitudes.reshape(peer_count, capacity, patch_size, patch_size)
    arrived = lax.all_to_all(sending, "scan", split_axis=0, concat_axis=0, tiled=True)
    grad_terms, probe_items = owner_work(arrived, measured, probe, tables)
    probe_sum = jnp.sum(probe_items, 0)
    returned = lax.all_to_all(grad_terms, "scan", split_axis=0, concat_axis=0, tiled=True)
    returned_flat = returned.reshape(peer_count * capacity, 2, patch_size, patch_size)
    gradient = jnp.zeros((2, rows_tile + patch_size, cols_tile + patch_size), jnp.float32)

    def add_slot(counter, accumulated):
        row_start = row_starts[counter]
        col_start = col_starts[counter]
        current = lax.dynamic_slice(
            accumulated, (anchor, row_start, col_start), (2, patch_size, patch_size)
        )
        return lax.dynamic_update_slice(
            accumulated,
            current + returned_flat[counter].astype(jnp.float32),
            (anchor, row_start, col_start),
        )

    gradient = lax.fori_loop(0, peer_count * capacity, add_slot, gradient)
    right_rim = passed_along(gradient[:, :, cols_tile:], "scan", 1)
    gradient = gradient.at[:, :, :patch_size].add(right_rim)
    lower_rim = passed_along(gradient[:, rows_tile:, :cols_tile], "obj", 1)
    object_grad = gradient[:, :rows_tile, :cols_tile].at[:, :patch_size, :].add(lower_rim)
    slot_total = band_count * peer_count * capacity
    probe_grad = lax.psum(probe_sum, "obj") / math.sqrt(slot_total)
    return (object_grad, probe_grad[None])


def solution(mesh):
    return jax.shard_map(
        on_device,
        mesh=mesh,
        in_specs=(
            P(None, "obj", "scan"),
            P(),
            P("obj", "scan", None, None),
            P("obj", "scan", None),
            P("obj", "scan", None),
        ),
        out_specs=(P(None, "obj", "scan"), P("scan", None, None, None)),
        check_vma=False,
    )
```

profile of v0, /device:TPU:1, one launch (start us, length us, event | category | flops | bytes accessed | tf_op | source)
XLA Modules:
  0.0 1137.5 jit_solution(4174270700507717113)
XLA Ops:
  10.3 13.8 %collective-permute-done = bf16[2,512,256]{2,1,0:T(8,128)(2,1)S(1)} collective-permute-done((bf16[2,512,256]{2,1,0:T(8,128)(2,1)S(1)}, bf16[2,512,256]{2,1,0:T(8,128)(2,1)S(1)}, u32[]{:S(2)}, u32[]{:S(2)}) %collective-permute-start) | collective-permute-done | bytes 524320 | tf_op jit(solution)/shard_map/ppermute | solution.py:12
  24.1 3.6 collective-permute-start.1
  28.4 10.6 collective-permute-done.1
  40.4 88.2 %while.32 = (s32[]{:T(128)}, bf16[2,768,768]{2,1,0:T(8,128)(2,1)S(1)}, s32[32,3]{0,1:T(4,128)S(1)}, bf16[32,2,256,256]{3,2,1,0:T(8,128)(2,1)}, s32[]{:T(128)}) while((s32[]{:T(128)}, bf16[2,768,768]{2,1,0:T(8,128)(2,1)S(1)}, s32[32,3]{0,1:T(4,128)S(1)}, bf16[32,2,256,256]{3,2,1,0:T(8,128)(2,1)}, s32[]{:T(128)}) %tuple.98), condition=%wide.while_cond.2, body=%wide.while_body.2.sunk | while | flops 2 | bytes 525929 | solution.py:107
  49.2 2.2 bitcast_dynamic-update-slice_fusion.5
  52.0 2.2 bitcast_dynamic-update-slice_fusion.5
  60.3 2.2 bitcast_dynamic-update-slice_fusion.5
  63.0 2.2 bitcast_dynamic-update-slice_fusion.5
  65.8 2.2 bitcast_dynamic-update-slice_fusion.5
  68.5 2.2 bitcast_dynamic-update-slice_fusion.5
  96.1 2.2 bitcast_dynamic-update-slice_fusion.5
  98.8 2.2 bitcast_dynamic-update-slice_fusion.5
  101.6 2.2 bitcast_dynamic-update-slice_fusion.5
  104.4 2.2 bitcast_dynamic-update-slice_fusion.5
  109.9 2.2 bitcast_dynamic-update-slice_fusion.5
  112.6 2.2 bitcast_dynamic-update-slice_fusion.5
  123.6 2.2 bitcast_dynamic-update-slice_fusion.5
  126.4 2.2 bitcast_dynamic-update-slice_fusion.5
  128.6 7.2 broadcast_select_fusion
  135.8 9.3 all-to-all-start
  154.8 95.8 %all-to-all-done = bf16[16,2,2,256,256]{4,3,2,1,0:T(8,128)(2,1)} async-done(((bf16[16,2,2,256,256]{4,3,2,1,0:T(8,128)(2,1)}), bf16[16,2,2,256,256]{4,3,2,1,0:T(8,128)(2,1)}, u32[]{:S(2)}, u32[]{:S(2)}) %all-to-all-start) | async-done | bytes 8388640 | tf_op jit(solution)/shard_map/all_to_all | solution.py:115
  250.5 194.8 %while.30 = (s32[]{:T(128)}, bf16[16,2,2,256,256]{4,3,1,2,0:T(8,128)(2,1)}, f32[16,2,256,256]{3,2,1,0:T(8,128)}, f32[2,256,256]{2,1,0:T(8,128)}, bf16[16,2,2,256...) while((s32[]{:T(128)}, ...), condition=%wide.region_2.3_spmd, body=%wide.region_0.2_spmd.sunk | while | flops 1081344000 | bytes 24380588 | solution.py:82
  445.3 4.8 all-to-all-start.1
  450.5 121.4 %all-to-all-done.1 = bf16[16,2,2,256,256]{4,3,1,2,0:T(8,128)(2,1)} async-done(((bf16[16,2,2,256,256]{4,3,1,2,0:T(8,128)(2,1)}), bf16[16,2,2,256,256]{4,3,1,2,0:T(8,128)(2,1)}, u32[]{:S(2)}, u32[]{:S(2)}) %all-to-all-start.1) | async-done | bytes 8388640 | tf_op jit(solution)/shard_map/all_to_all | solution.py:118
  572.0 7.6 copy.46
  579.6 2.5 broadcast_in_dim.38
  582.1 409.5 %while.31 = (s32[]{:T(128)}, f32[2,768,768]{2,1,0:T(8,128)}, s32[32]{0:T(128)S(1)}, s32[32]{0:T(128)S(1)}, bf16[32,2,256,256]{3,2,1,0:T(8,128)(2,1)}, /*index=5*/s32[]{:T(128)}, s32[]{:T(128)}, s32[]{:T(128)}) while((s32[]{:T(128)}, f32[2,768,768]{2,1,0:T(8,128)}, s32[32]{0:T(128)S(1)}, s32[32]{0:T(128)S(1)}, ...), condition=%wide.region_4.5_spmd, body=%wide.region_3.4_spmd.sunk | while | flops 262152 | bytes 2359489 | solution.py:134
  588.6 6.6 dynamic_update_slice.28
  601.6 6.3 dynamic_update_slice.28
  614.5 5.9 dynamic_update_slice.28
  626.9 5.9 dynamic_update_slice.28
  639.3 6.8 dynamic_update_slice.28
  652.6 6.8 dynamic_update_slice.28
  665.8 5.9 dynamic_update_slice.28
  678.3 5.9 dynamic_update_slice.28
  690.7 5.9 dynamic_update_slice.28
  703.1 5.9 dynamic_update_slice.28
  715.5 6.3 dynamic_update_slice.28
  728.3 6.6 dynamic_update_slice.28
  741.4 6.6 dynamic_update_slice.28
  754.5 6.8 dynamic_update_slice.28
  767.7 6.5 dynamic_update_slice.28
  780.7 6.8 dynamic_update_slice.28
  794.0 6.6 dynamic_update_slice.28
  807.0 5.9 dynamic_update_slice.28
  819.4 6.8 dynamic_update_slice.28
  832.7 5.9 dynamic_update_slice.28
  845.1 6.6 dynamic_update_slice.28
  858.2 6.7 dynamic_update_slice.28
  871.4 6.4 dynamic_update_slice.28
  884.3 5.9 dynamic_update_slice.28
  896.7 6.8 dynamic_update_slice.28
  909.9 5.9 dynamic_update_slice.28
  922.4 6.3 dynamic_update_slice.28
  935.1 5.9 dynamic_update_slice.28
  947.6 5.9 dynamic_update_slice.28
  960.0 5.9 dynamic_update_slice.28
  972.4 6.7 dynamic_update_slice.28
  985.6 5.9 dynamic_update_slice.28
  994.5 32.3 %collective-permute-done.2 = f32[2,768,256]{2,1,0:T(8,128)S(1)} collective-permute-done((f32[2,768,256]{2,1,0:T(8,128)S(1)}, f32[2,768,256]{2,1,0:T(8,128)S(1)}, u32[]{:S(2)}, u32[]{:S(2)}) %collective-permute-start.2) | collective-permute-done | bytes 1572896 | tf_op jit(solution)/shard_map/ppermute | solution.py:12
  1026.8 2.9 add_dynamic-update-slice_fusion
  1031.0 27.7 %collective-permute-start.3 = (f32[2,256,512]{2,1,0:T(8,128)S(1)}, f32[2,256,512]{2,1,0:T(8,128)S(1)}, u32[]{:S(2)}, u32[]{:S(2)}) collective-permute-start(f32[2,256,512]{2,1,0:T(8,128)S(1)} %slice.163), channel_id=1, source_target_pairs={{0,16},{16,32},{32,48},{48,64},{64,80},{80,96},{96,112},{1,17},{17... | collective-permute-start | bytes 3145736 | tf_op jit(solution)/shard_map/ppermute | solution.py:12
  1058.7 4.8 reduce_sum.21
  1063.6 60.7 %all-reduce.2.cloned.1.call-done = f32[2,256,256]{2,1,0:T(8,128)} async-done(((f32[2,256,256]{2,1,0:T(8,128)}), f32[2,256,256]{2,1,0:T(8,128)}) %all-reduce.2.cloned.1.call-update) | async-done | bytes 524304 | tf_op jit(solution)/shard_map/psum | solution.py:140
  (467 shorter events, 360.3 us)
Async XLA Ops:
  7.2 20.6 %copy-start.5 = (s32[1,16,2]{1,2,0:T(2,128)S(1)}, s32[1,16,2]{1,2,0:T(2,128)}, u32[]{:S(2)}) copy-start(s32[1,16,2]{1,2,0:T(2,128)} %param.16) | copy-start | bytes 388
  7.2 20.8 %copy-start.4 = (s32[1,16,2]{1,2,0:T(2,128)S(1)}, s32[1,16,2]{1,2,0:T(2,128)}, u32[]{:S(2)}) copy-start(s32[1,16,2]{1,2,0:T(2,128)} %param.17) | copy-start | bytes 388
  9.0 15.1 %collective-permute-start = (bf16[2,512,256]{2,1,0:T(8,128)(2,1)S(1)}, bf16[2,512,256]{2,1,0:T(8,128)(2,1)S(1)}, u32[]{:S(2)}, u32[]{:S(2)}) collective-permute-start(bf16[2,512,256]{2,1,0:T(8,128)(2,1)S(1)} %slice.160), channel_id=1, source_target_pairs={{1,0},{2,1},{3,2},{4,3},{5,4},{6,5},{7,6},{8,7},{9,8},{10,9},{11,1... | collective-permute-start | bytes 1572872 | tf_op jit(solution)/shard_map/ppermute | solution.py:12
  24.1 4.3 copy-start.3
  24.1 14.8 %collective-permute-start.1 = (bf16[2,256,768]{2,1,0:T(8,128)(2,1)S(1)}, bf16[2,256,768]{2,1,0:T(8,128)(2,1)}, u32[]{:S(2)}, u32[]{:S(2)}) collective-permute-start(bf16[2,256,768]{2,1,0:T(8,128)(2,1)S(1)} %pad_maximum_fusion.1), channel_id=1, source_target_pairs={{16,0},{32,16},{48,32},{64,48},{80,64},{96,80},{112,96},{17,1},{33... | collective-permute-start | bytes 2359304 | tf_op jit(solution)/shard_map/ppermute | solution.py:12
  135.8 114.7 %all-to-all-start = ((bf16[16,2,2,256,256]{4,3,2,1,0:T(8,128)(2,1)}), bf16[16,2,2,256,256]{4,3,2,1,0:T(8,128)(2,1)}, u32[]{:S(2)}, u32[]{:S(2)}) async-start(bf16[16,2,2,256,256]{4,3,2,1,0:T(8,128)(2,1)} %broadcast_select_fusion), calls=%async_computation | async-start | bytes 16777216 | tf_op jit(solution)/shard_map/all_to_all | solution.py:115
  252.7 0.7 copy-start
  259.6 2.1 copy-start.1
  264.9 0.7 copy-start
  271.8 2.2 copy-start.1
  277.1 0.7 copy-start
  283.9 2.2 copy-start.1
  289.3 0.7 copy-start
  296.1 2.2 copy-start.1
  301.4 0.7 copy-start
  308.3 2.2 copy-start.1
  313.6 0.7 copy-start
  320.5 2.1 copy-start.1
  325.8 0.7 copy-start
  332.6 2.1 copy-start.1
  337.9 0.7 copy-start
  344.8 2.1 copy-start.1
  350.1 0.7 copy-start
  356.9 2.1 copy-start.1
  362.3 0.7 copy-start
  369.1 2.2 copy-start.1
  374.4 0.7 copy-start
  381.3 2.2 copy-start.1
  386.6 0.7 copy-start
  393.5 2.2 copy-start.1
  398.8 0.7 copy-start
  405.6 2.1 copy-start.1
  410.9 0.7 copy-start
  417.8 2.1 copy-start.1
  423.1 0.7 copy-start
  429.9 2.1 copy-start.1
  435.3 0.7 copy-start
  442.1 2.2 copy-start.1
  445.3 126.7 %all-to-all-start.1 = ((bf16[16,2,2,256,256]{4,3,1,2,0:T(8,128)(2,1)}), bf16[16,2,2,256,256]{4,3,1,2,0:T(8,128)(2,1)}, u32[]{:S(2)}, u32[]{:S(2)}) async-start(bf16[16,2,2,256,256]{4,3,1,2,0:T(8,128)(2,1)} %get-tuple-element.246), calls=%async_computation.1 | async-start | bytes 16777216 | tf_op jit(solution)/shard_map/all_to_all | solution.py:118
  450.1 674.1 %all-reduce.2.cloned.1.call-start = ((), (), s32[]{:S(2)}) async-start(), calls=%async_computation.2 | async-start | bytes 1048576 | tf_op jit(solution)/shard_map/psum | solution.py:140
  993.1 33.7 %collective-permute-start.2 = (f32[2,768,256]{2,1,0:T(8,128)S(1)}, f32[2,768,256]{2,1,0:T(8,128)S(1)}, u32[]{:S(2)}, u32[]{:S(2)}) collective-permute-start(f32[2,768,256]{2,1,0:T(8,128)S(1)} %slice.135), channel_id=1, source_target_pairs={{0,1},{1,2},{2,3},{3,4},{4,5},{5,6},{6,7},{7,8},{8,9},{9,10},{10,1... | collective-permute-start | bytes 4718600 | tf_op jit(solution)/shard_map/ppermute | solution.py:12
  1031.0 96.9 %collective-permute-start.3 = (f32[2,256,512]{2,1,0:T(8,128)S(1)}, f32[2,256,512]{2,1,0:T(8,128)S(1)}, u32[]{:S(2)}, u32[]{:S(2)}) collective-permute-start(f32[2,256,512]{2,1,0:T(8,128)S(1)} %slice.163), channel_id=1, source_target_pairs={{0,16},{16,32},{32,48},{48,64},{64,80},{80,96},{96,112},{1,17},{17... | collective-permute-start | bytes 3145736 | tf_op jit(solution)/shard_map/ppermute | solution.py:12
  1129.3 1.3 copy-start.2
Sparse Core Ops, SparseCore 0:
  1063.7 60.5 all-reduce.1
where the time goes:
time: 1150 us; the launch traced here: 1140 us
  local copies, waits for them, and re-layouts  387 us (34%)
  waiting for transfers between devices  335 us (29%)
  other arithmetic  162 us (14%)
  loops' own time  126 us (11%)
  matrix products  65 us (6%)
  starting transfers between devices  48.4 us (4%)
  between operations  14.3 us (1%)
    dynamic_update_slice x32, local copies, waits for them, and re-layouts, add_slot(): lax.dynamic_update_slice(accumulated, current + returned_flat[counter].as...  202 us
    another operation x1, loops' own time, on_device(): gradient = lax.fori_loop(0, peer_count * capacity, add_slot, gradient)  125 us
    all_to_all x1, waiting for transfers between devices, on_device(): lax.all_to_all(grad_terms, 'scan', split_axis=0, concat_axis=0, tiled=True)  121 us
    all_to_all x1, waiting for transfers between devices, on_device(): lax.all_to_all(sending, 'scan', split_axis=0, concat_axis=0, tiled=True)  95.8 us
    gather x96, local copies, waits for them, and re-layouts  88.1 us
    psum x1, waiting for transfers between devices, on_device(): probe_grad = lax.psum(probe_sum, 'obj') / math.sqrt(slot_total)  60.7 us
    ppermute x4, waiting for transfers between devices, passed_along(): return lax.ppermute(shard, axis, pairs)  56.7 us
    add x32, other arithmetic, add_slot(): current + returned_flat[counter].astype(jnp.float32)  45.5 us
  transfers between devices with their start and end apart: 7, of which 6 were waited for; matrix products, arithmetic and copies ran while one was open for 2% of the time, Pallas kernels for 0%

commit v1 on v0

v1 whole, which is shorter than its diff:
```python
import functools
import math

import jax
import jax.numpy as jnp
import ml_dtypes
import numpy as np
from jax import lax
from jax.experimental import pallas as pl
from jax.experimental.pallas import tpu as pltpu
from jax.sharding import PartitionSpec as P

MESH = pl.DeviceIdType.MESH
F32 = jnp.float32
BF16 = jnp.bfloat16

ORDER = [
    (0, 0), (1, 1), (3, 3), (1, 3), (3, 1), (0, 1), (1, 0), (0, 3),
    (3, 0), (2, 2), (1, 2), (2, 1), (3, 2), (2, 3), (0, 2), (2, 0),
]
CODES = [dz * 4 + dx for dz, dx in ORDER]
RP = 32
CH = 32
EC = 32


def dft_tables(length):
    grid = np.arange(length)
    angle = 2.0 * math.pi / length * (grid[:, None] * grid[None, :] % length)
    real = np.cos(angle) / math.sqrt(length)
    imag = -np.sin(angle) / math.sqrt(length)
    left = np.block([[real, -imag], [imag, real]])
    right = np.block([[real, imag], [-imag, real]])
    return left.astype(ml_dtypes.bfloat16), right.astype(ml_dtypes.bfloat16)


def code_of(n):
    return functools.reduce(lambda a, t: jnp.where(n == t, CODES[t], a), range(1, 16), jnp.int32(0))


def kernel(
    row_ref, col_ref, obj, probe, amps, ltab, rtab,
    out, pout,
    amp, ext, grad, term, patch, ebuf, hbuf, dbuf, bbuf, wide, pacc,
    strip_s, strip_r, low_s, low_r, corner_r,
    sib_s, sib_r, ysum, y_s, y_r, q_s, q_r, pg,
    rim_s, rim_r, lrim_s, lrim_r, crim_r,
    local_sem, halo_ss, halo_rs, amp_ss, amp_rs, sib_ss, sib_rs, y_ss, y_rs, q_ss, q_rs, g_ss, g_rs, rim_ss, rim_rs,
):
    me = lax.axis_index("scan")
    band = lax.axis_index("obj")
    z, x = me // 4, me % 4
    yy, core = band // 2, band % 2
    left, right = (me + 15) % 16, (me + 1) % 16
    above, below = (band + 7) % 8, (band + 1) % 8

    barrier = pltpu.get_barrier_semaphore()
    for d in range(1, 16):
        pl.semaphore_signal(barrier, inc=1, device_id={"scan": (me + d) % 16}, device_id_type=MESH)
    for d in range(1, 8):
        pl.semaphore_signal(barrier, inc=1, device_id={"obj": (band + d) % 8}, device_id_type=MESH)

    def remote(src, dst, ss, rs, where):
        return pltpu.make_async_remote_copy(
            src_ref=src, dst_ref=dst, send_sem=ss, recv_sem=rs, device_id=where, device_id_type=MESH
        )

    tile_in = []
    for p in range(2):
        for b in range(4):
            cp = pltpu.make_async_copy(
                obj.at[p, :, pl.ds(b * 128, 128)], ext.at[p, b, pl.ds(0, 512)], local_sem.at[p * 4 + b]
            )
            cp.start()
            tile_in.append(cp)
    own_in = []
    for s in range(2):
        cp = pltpu.make_async_copy(amps.at[2 * me + s], amp.at[s * 16], local_sem.at[8 + s])
        cp.start()
        own_in.append(cp)
    for cp in tile_in:
        cp.wait()

    def round_rows(i, c):
        rows = pl.ds(pl.multiple_of(i * 64, 64), 64)
        for p in range(2):
            for b in range(4):
                v = ext[p, b, rows, :].astype(BF16)
                ext[p, b, rows, :] = v.astype(F32)
                if b < 2:
                    strip_s[p, b, rows, :] = v
        return c

    lax.fori_loop(0, 8, round_rows, 0)

    def low_rows(i, c):
        rows = pl.ds(pl.multiple_of(i * 64, 64), 64)
        for p in range(2):
            for b in range(4):
                low_s[p, b, rows, :] = ext[p, b, rows, :].astype(BF16)
        return c

    lax.fori_loop(0, 4, low_rows, 0)

    pl.semaphore_wait(barrier, 22)

    strip_cp = remote(strip_s, strip_r, halo_ss.at[0], halo_rs.at[0], {"scan": left})
    strip_cp.start()
    low_cp = remote(low_s, low_r, halo_ss.at[1], halo_rs.at[1], {"obj": above})
    low_cp.start()

    def amp_copy(t, s):
        dz, dx = ORDER[t]
        target = ((z + dz) % 4) * 4 + (x + dx) % 4
        at = s * 16 + CODES[t]
        return remote(amps.at[2 * target + s], amp.at[at], amp_ss.at[at], amp_rs.at[at], {"scan": target})

    for s in range(2):
        for t in range(1, 16):
            amp_copy(t, s).start()

    def zero_rows(i, c):
        rows = pl.ds(pl.multiple_of(i * 64, 64), 64)
        nil = jnp.zeros((64, 128), F32)
        for p in range(2):
            for b in range(3):
                ext[p, 6 + b, rows, :] = nil
            for b in range(6):
                grad[p, b, rows, :] = nil
        return c

    lax.fori_loop(0, 12, zero_rows, 0)

    def zero_terms(i, c):
        nil = jnp.zeros((RP, 128), F32)
        term[i, 0:RP, :] = nil
        term[i, RP + 256 : RP + 256 + RP, :] = nil
        return c

    lax.fori_loop(0, 24, zero_terms, 0)
    term[24] = jnp.zeros((256 + 2 * RP, 128), F32)

    strip_cp.wait_recv()
    corner_cp = remote(
        strip_r.at[:, :, pl.ds(0, 256)], corner_r, halo_ss.at[2], halo_rs.at[2], {"obj": above}
    )
    corner_cp.start()

    def strip_rows(i, c):
        rows = pl.ds(pl.multiple_of(i * 64, 64), 64)
        for p in range(2):
            for b in range(2):
                ext[p, 4 + b, rows, :] = strip_r[p, b, rows, :].astype(F32)
        return c

    lax.fori_loop(0, 8, strip_rows, 0)
    low_cp.wait_recv()

    def low_in(i, c):
        rows = pl.ds(pl.multiple_of(i * 64, 64), 64)
        dest = pl.ds(pl.multiple_of(512 + i * 64, 64), 64)
        for p in range(2):
            for b in range(4):
                ext[p, b, dest, :] = low_r[p, b, rows, :].astype(F32)
        return c

    lax.fori_loop(0, 4, low_in, 0)
    corner_cp.wait_recv()

    def corner_in(i, c):
        rows = pl.ds(pl.multiple_of(i * 64, 64), 64)
        dest = pl.ds(pl.multiple_of(512 + i * 64, 64), 64)
        for p in range(2):
            for b in range(2):
                ext[p, 4 + b, dest, :] = corner_r[p, b, rows, :].astype(F32)
        return c

    lax.fori_loop(0, 4, corner_in, 0)
    for cp in own_in:
        cp.wait()

    lane = lax.broadcasted_iota(jnp.int32, (EC, 128), 1)

    def owner_of(n):
        code = code_of(n)
        dz, dx = code // 4, code % 4
        return code, ((z + 4 - dz) % 4) * 4 + (x + 4 - dx) % 4

    def pair(s, i, u):
        slots = []
        for a in range(2):
            code, owner = owner_of(2 * i + a)
            at = s * 16 + code
            if a == 0:

                @pl.when(i > 0)
                def _():
                    pltpu.make_async_remote_copy(
                        src_ref=amp.at[at], dst_ref=amp.at[at], send_sem=amp_ss.at[at], recv_sem=amp_rs.at[at],
                        device_id={"scan": right}, device_id_type=MESH,
                    ).wait_recv()
            else:
                pltpu.make_async_remote_copy(
                    src_ref=amp.at[at], dst_ref=amp.at[at], send_sem=amp_ss.at[at], recv_sem=amp_rs.at[at],
                    device_id={"scan": right}, device_id_type=MESH,
                ).wait_recv()
            row = row_ref[owner * 2 + s]
            col = col_ref[owner * 2 + s]
            live = row >= 0
            r0 = jnp.maximum(row, 0)
            c0 = jnp.maximum(col, 0)
            block = jnp.where(live, c0 // 128, 6)
            slots.append((at, r0, block, c0 % 128))
        for a, (at, r0, block, shift) in enumerate(slots):
            for rc in range(0, 256, EC):
                f = []
                for p in range(2):
                    raw = [
                        pltpu.roll(ext[p, block + q, pl.ds(r0 + rc, EC), :], (128 - shift) % 128, 1) for q in range(3)
                    ]
                    f.append([jnp.where(lane < 128 - shift, raw[b], raw[b + 1]) for b in range(2)])
                for b in range(2):
                    lanes = slice(b * 128, b * 128 + 128)
                    fr, fi = f[0][b], f[1][b]
                    pr, pi = probe[0, rc : rc + EC, lanes], probe[1, rc : rc + EC, lanes]
                    patch[a, 0, rc : rc + EC, lanes] = fr.astype(BF16)
                    patch[a, 1, rc : rc + EC, lanes] = fi.astype(BF16)
                    here = slice(a * 256 + b * 128, a * 256 + b * 128 + 128)
                    ebuf[rc : rc + EC, here] = (pr * fr - pi * fi).astype(BF16)
                    ebuf[256 + rc : 256 + rc + EC, here] = (pr * fi + pi * fr).astype(BF16)
        half = jnp.dot(ltab[...], ebuf[...], preferred_element_type=F32).astype(BF16)
        for a in range(2):
            for p in range(2):
                hbuf[a * 256 : a * 256 + 256, p * 256 : p * 256 + 256] = half[
                    p * 256 : p * 256 + 256, a * 256 : a * 256 + 256
                ]
        wide[...] = jnp.dot(hbuf[...], rtab[...], preferred_element_type=F32)
        for a, (at, r0, block, shift) in enumerate(slots):
            for rc in range(0, 256, EC):
                fr = wide[a * 256 + rc : a * 256 + rc + EC, 0:256]
                fi = wide[a * 256 + rc : a * 256 + rc + EC, 256:512]
                m = amp[at, rc : rc + EC, :].astype(F32)
                scale = m * lax.rsqrt(jnp.maximum(fr * fr + fi * fi, 0.01)) - 1.0
                dbuf[rc : rc + EC, a * 256 : a * 256 + 256] = (fr * scale).astype(BF16)
                dbuf[256 + rc : 256 + rc + EC, a * 256 : a * 256 + 256] = (fi * scale).astype(BF16)
        back = jnp.dot(rtab[...], dbuf[...], preferred_element_type=F32).astype(BF16)
        for a in range(2):
            for p in range(2):
                bbuf[a * 256 : a * 256 + 256, p * 256 : p * 256 + 256] = back[
                    p * 256 : p * 256 + 256, a * 256 : a * 256 + 256
                ]
        wide[...] = jnp.dot(bbuf[...], ltab[...], preferred_element_type=F32)
        for a, (at, r0, block, shift) in enumerate(slots):
            base = (u * 2 + a) * 6
            n = 2 * i + a
            for rc in range(0, 256, EC):
                rows = slice(rc, rc + EC)
                trail = [None, None]
                for b in range(2):
                    lanes = slice(b * 128, b * 128 + 128)
                    nr = wide[a * 256 + rc : a * 256 + rc + EC, b * 128 : b * 128 + 128]
                    ni = wide[a * 256 + rc : a * 256 + rc + EC, 256 + b * 128 : 256 + b * 128 + 128]
                    pr, pi = probe[0, rows, lanes], probe[1, rows, lanes]
                    fr, fi = patch[a, 0, rows, lanes].astype(F32), patch[a, 1, rows, lanes].astype(F32)
                    tt = (pr * nr + pi * ni, pr * ni - pi * nr)
                    for p in range(2):
                        turned = pltpu.roll(tt[p], shift, 1)
                        before = trail[p] if b else jnp.zeros_like(turned)
                        term[base + p * 3 + b, RP + rc : RP + rc + EC, :] = jnp.where(lane >= shift, turned, before)
                        trail[p] = turned
                    pacc[n, 0, rows, lanes] = jnp.where(s == 0, 0.0, pacc[n, 0, rows, lanes]) + (fr * nr + fi * ni)
                    pacc[n, 1, rows, lanes] = jnp.where(s == 0, 0.0, pacc[n, 1, rows, lanes]) + (fr * ni - fi * nr)
                for p in range(2):
                    term[base + p * 3 + 2, RP + rc : RP + rc + EC, :] = jnp.where(
                        lane >= shift, jnp.zeros_like(trail[p]), trail[p]
                    )

    def gather(s, v):
        places = []
        for w in range(4):
            code, owner = owner_of(4 * v + w)
            row = jnp.maximum(row_ref[owner * 2 + s], 0)
            block = jnp.maximum(col_ref[owner * 2 + s], 0) // 128
            places.append((row, block))
        picks = [
            [
                [
                    jnp.where((b - block >= 0) & (b - block < 3), (w * 2 + p) * 3 + b - block, 24)
                    for w, (row, block) in enumerate(places)
                ]
                for b in range(6)
            ]
            for p in range(2)
        ]

        def rows_of(ic, c):
            rows = pl.ds(pl.multiple_of(ic * CH, CH), CH)
            starts = [jnp.clip(ic * CH - row, -RP, 256) + RP for row, block in places]
            for b in range(6):
                for p in range(2):
                    acc = grad[p, b, rows, :]
                    for w in range(4):
                        acc = acc + term[picks[p][b][w], pl.ds(starts[w], CH), :]
                    grad[p, b, rows, :] = acc
            return c

        lax.fori_loop(0, 768 // CH, rows_of, 0)

    def sib_copy(i):
        return remote(sib_s.at[i], sib_r.at[i], sib_ss.at[i], sib_rs.at[i], {"obj": 2 * yy + 1 - core})

    def y_copy(i, d):
        to = (yy + d) % 4
        return remote(
            y_s.at[i, to], y_r.at[i, d - 1], y_ss.at[i * 3 + d - 1], y_rs.at[i * 3 + d - 1], {"obj": 2 * to + core}
        )

    def q_copy(i, a):
        code, owner = owner_of(2 * i + a)
        return remote(q_s.at[i, a], q_r.at[code], q_ss.at[code], q_rs.at[code], {"scan": owner})

    mine = pl.ds(pl.multiple_of(core * 128, 128), 128)
    other = pl.ds(pl.multiple_of((1 - core) * 128, 128), 128)

    def sib_stage(i):
        for a in range(2):
            for p in range(2):
                sib_s[i, a, p] = pacc[2 * i + a, p, other, :].astype(BF16)
        sib_copy(i).start()

    def y_stage(i):
        sib_copy(i).wait_recv()
        for a in range(2):
            for p in range(2):
                total = pacc[2 * i + a, p, mine, :] + sib_r[i, a, p].astype(F32)
                for q in range(4):
                    ysum[i, q, a, p] = total[q * 32 : q * 32 + 32]
                    y_s[i, q, a, p] = total[q * 32 : q * 32 + 32].astype(BF16)
        for d in range(1, 4):
            y_copy(i, d).start()

    def q_stage(i):
        for d in range(1, 4):
            y_copy(i, d).wait_recv()
        for a in range(2):
            for p in range(2):
                total = ysum[i, yy, a, p]
                for d in range(3):
                    total = total + y_r[i, d, a, p].astype(F32)
                q_s[i, a, p] = total.astype(BF16)

        @pl.when(i > 0)
        def _():
            q_copy(i, 0).start()

        q_copy(i, 1).start()

    def double_step(v2, c):
        s, v = v2 // 4, v2 % 4

        def single(u, c):
            i = 2 * v + u

            @pl.when((s == 1) & (i >= 1))
            def _():
                y_stage(i - 1)

            @pl.when((s == 1) & (i >= 2))
            def _():
                q_stage(i - 2)

            pair(s, i, u)

            @pl.when(s == 1)
            def _():
                sib_stage(i)

            return c

        lax.fori_loop(0, 2, single, 0)
        gather(s, v)
        return c

    lax.fori_loop(0, 8, double_step, 0)

    def corner_out(i, c):
        rows = pl.ds(pl.multiple_of(i * 64, 64), 64)
        low = pl.ds(pl.multiple_of(512 + i * 64, 64), 64)
        for p in range(2):
            for b in range(6):
                lrim_s[(b + 2) % 6 // 2, p, b % 2, rows, :] = grad[p, b, low, :].astype(BF16)
        return c

    lax.fori_loop(0, 4, corner_out, 0)
    crim_cp = remote(lrim_s.at[0], crim_r, rim_ss.at[0], rim_rs.at[0], {"obj": below})
    crim_cp.start()

    def rim_low_half(i, c):
        rows = pl.ds(pl.multiple_of(i * 64, 64), 64)
        src = pl.ds(pl.multiple_of(256 + i * 64, 64), 64)
        for p in range(2):
            for b in range(2):
                rim_s[1, p, b, rows, :] = grad[p, 4 + b, src, :].astype(BF16)
        return c

    lax.fori_loop(0, 4, rim_low_half, 0)
    rim_b = remote(rim_s.at[1], rim_r.at[1], rim_ss.at[1], rim_rs.at[1], {"scan": right})
    rim_b.start()
    lrim_cp = remote(lrim_s.at[pl.ds(1, 2)], lrim_r, rim_ss.at[2], rim_rs.at[2], {"obj": below})
    lrim_cp.start()
    y_stage(7)
    q_stage(6)
    crim_cp.wait_recv()

    def rim_top_half(i, c):
        rows = pl.ds(pl.multiple_of(i * 64, 64), 64)
        for p in range(2):
            for b in range(2):
                rim_s[0, p, b, rows, :] = (grad[p, 4 + b, rows, :] + crim_r[p, b, rows, :].astype(F32)).astype(BF16)
        return c

    lax.fori_loop(0, 4, rim_top_half, 0)
    rim_t = remote(rim_s.at[0], rim_r.at[0], rim_ss.at[3], rim_rs.at[3], {"scan": right})
    rim_t.start()
    q_stage(7)

    def out_copy(p, b, h):
        rows = pl.ds(h * 256, 256)
        return pltpu.make_async_copy(
            grad.at[p, b, rows], out.at[p, rows, pl.ds(b * 128, 128)], local_sem.at[(p * 4 + b) * 2 + h]
        )

    for p in range(2):
        for b in range(2, 4):
            out_copy(p, b, 1).start()

    for n in range(1, 16):
        code = CODES[n]
        remote(q_s.at[0, 0], q_r.at[code], q_ss.at[code], q_rs.at[code], {"scan": right}).wait_recv()
    piece = core * 4 + yy
    prow = pl.ds(pl.multiple_of(piece * 32, 32), 32)
    for p in range(2):
        total = q_s[0, 0, p].astype(F32)
        for n in range(1, 16):
            total = total + q_r[CODES[n], p].astype(F32)
        pg[p, prow, :] = total * (1.0 / 16.0)

    def g_copy(d):
        to = (band + d) % 8
        return remote(pg.at[:, prow], pg.at[:, prow], g_ss.at[d - 1], g_rs.at[d - 1], {"obj": to})

    for d in range(1, 8):
        g_copy(d).start()

    lrim_cp.wait_recv()

    def add_low(i, c):
        rows = pl.ds(pl.multiple_of(i * 64, 64), 64)
        for p in range(2):
            for b in range(4):
                grad[p, b, rows, :] = grad[p, b, rows, :] + lrim_r[b // 2, p, b % 2, rows, :].astype(F32)
        return c

    lax.fori_loop(0, 4, add_low, 0)
    for p in range(2):
        for b in range(2, 4):
            out_copy(p, b, 0).start()
    for h, cp in ((1, rim_b), (0, rim_t)):
        cp.wait_recv()

        def add_rim(i, c):
            rows = pl.ds(pl.multiple_of(i * 64, 64), 64)
            dest = pl.ds(pl.multiple_of(h * 256 + i * 64, 64), 64)
            for p in range(2):
                for b in range(2):
                    grad[p, b, dest, :] = grad[p, b, dest, :] + rim_r[h, p, b, rows, :].astype(F32)
            return c

        lax.fori_loop(0, 4, add_rim, 0)
        for p in range(2):
            for b in range(2):
                out_copy(p, b, h).start()

    for d in range(1, 8):
        frm = (band + 8 - d) % 8
        frow = pl.ds(pl.multiple_of(((frm % 2) * 4 + frm // 2) * 32, 32), 32)
        remote(pg.at[:, frow], pg.at[:, frow], g_ss.at[d - 1], g_rs.at[d - 1], {"obj": frm}).wait_recv()
    pcp = pltpu.make_async_copy(pg, pout, local_sem.at[16])
    pcp.start()

    for cp in (strip_cp, low_cp, corner_cp, crim_cp, rim_b, lrim_cp, rim_t):
        cp.wait_send()
    for s in range(2):
        for t in range(1, 16):
            amp_copy(t, s).wait_send()

    def drain(i, c):
        sib_copy(i).wait_send()
        for d in range(1, 4):
            y_copy(i, d).wait_send()

        @pl.when(i > 0)
        def _():
            q_copy(i, 0).wait_send()

        q_copy(i, 1).wait_send()
        return c

    lax.fori_loop(0, 8, drain, 0)
    for d in range(1, 8):
        g_copy(d).wait_send()
    for p in range(2):
        for b in range(4):
            for h in range(2):
                out_copy(p, b, h).wait()
    pcp.wait()


def on_device(object_field, probe, amplitudes, corner_row, corner_col):
    ltab, rtab = dft_tables(256)
    vm = pltpu.VMEM
    dma = pltpu.SemaphoreType.DMA
    anywhere = pl.BlockSpec(memory_space=pl.ANY)
    inside = pl.BlockSpec(memory_space=pltpu.VMEM)
    scalar = pl.BlockSpec(memory_space=pltpu.SMEM)
    object_grad, probe_grad = pl.pallas_call(
        kernel,
        out_shape=(
            jax.ShapeDtypeStruct((2, 512, 512), F32),
            jax.ShapeDtypeStruct((2, 256, 256), F32),
        ),
        in_specs=[scalar, scalar, anywhere, inside, anywhere, inside, inside],
        out_specs=(anywhere, anywhere),
        scratch_shapes=[
            vm((32, 256, 256), BF16),
            vm((2, 9, 768, 128), F32),
            vm((2, 6, 768, 128), F32),
            vm((25, 256 + 2 * RP, 128), F32),
            vm((2, 2, 256, 256), BF16),
            vm((512, 512), BF16),
            vm((512, 512), BF16),
            vm((512, 512), BF16),
            vm((512, 512), BF16),
            vm((512, 512), F32),
            vm((16, 2, 256, 256), F32),
            vm((2, 2, 512, 128), BF16),
            vm((2, 2, 512, 128), BF16),
            vm((2, 4, 256, 128), BF16),
            vm((2, 4, 256, 128), BF16),
            vm((2, 2, 256, 128), BF16),
            vm((8, 2, 2, 128, 256), BF16),
            vm((8, 2, 2, 128, 256), BF16),
            vm((8, 4, 2, 2, 32, 256), F32),
            vm((8, 4, 2, 2, 32, 256), BF16),
            vm((8, 3, 2, 2, 32, 256), BF16),
            vm((8, 2, 2, 32, 256), BF16),
            vm((16, 2, 32, 256), BF16),
            vm((2, 256, 256), F32),
            vm((2, 2, 2, 256, 128), BF16),
            vm((2, 2, 2, 256, 128), BF16),
            vm((3, 2, 2, 256, 128), BF16),
            vm((2, 2, 2, 256, 128), BF16),
            vm((2, 2, 256, 128), BF16),
            dma((17,)),
            dma((3,)), dma((3,)),
            dma((32,)), dma((32,)),
            dma((8,)), dma((8,)),
            dma((24,)), dma((24,)),
            dma((16,)), dma((16,)),
            dma((7,)), dma((7,)),
            dma((4,)), dma((4,)),
        ],
        compiler_params=pltpu.CompilerParams(
            collective_id=0, has_side_effects=True, vmem_limit_bytes=62 * 2**20
        ),
        cost_estimate=pl.CostEstimate(flops=32 * 16 * 2 * 256**3, bytes_accessed=10 * 2**20, transcendentals=32 * 65536),
    )(
        corner_row.reshape(32), corner_col.reshape(32), object_field, probe, amplitudes[0],
        jnp.asarray(ltab), jnp.asarray(rtab),
    )
    return object_grad, probe_grad[None]


def solution(mesh):
    return jax.shard_map(
        on_device,
        mesh=mesh,
        in_specs=(
            P(None, "obj", "scan"),
            P(),
            P("obj", "scan", None, None),
            P("obj", "scan", None),
            P("obj", "scan", None),
        ),
        out_specs=(P(None, "obj", "scan"), P("scan", None, None, None)),
        check_vma=False,
    )
```

time: 1150 us -> 135 us (0.12)
  local copies, waits for them, and re-layouts: 387 us -> 6.65 us
  waiting for transfers between devices: 335 us -> 0 us
  other arithmetic: 162 us -> 0 us
  Pallas kernels: 0 us -> 127 us
  loops' own time: 126 us -> 0 us
  matrix products: 65 us -> 0 us
  starting transfers between devices: 48.4 us -> 0 us
  between operations: 14.3 us -> 0.65 us
    all_to_all x2 -> x0, waiting for transfers between devices: 217 us -> none  [the longest x1 121 us: on_device(): lax.all_to_all(grad_terms, 'scan', split_axis=0, concat_axis=0, tiled=True)]
    dynamic_update_slice x48 -> x0, local copies, waits for them, and re-layouts: 216 us -> none  [the longest x32 202 us: add_slot(): lax.dynamic_update_slice(accumulated, current + returned_flat[counter].as...]
    pallas_call x0 -> x1, Pallas kernels: none -> 127 us  [on_device(): pl.pallas_call(kernel, out_shape=(jax.ShapeDtypeStruct((2, 512, 512), F32...]
    another operation x3 -> x0, loops' own time: 126 us -> none  [the longest x1 125 us: on_device(): gradient = lax.fori_loop(0, peer_count * capacity, add_slot, gradient)]
    gather x96 -> x0, local copies, waits for them, and re-layouts: 88.1 us -> none
    dot_general x32 -> x0, matrix products: 65 us -> none  [the longest x16 34 us: slot_block(): jnp.einsum('sauy,aycv->scuv', back_half, inv_right, preferred_element_typ...]
    add x48 -> x0, other arithmetic: 64.9 us -> none  [the longest x32 45.5 us: add_slot(): current + returned_flat[counter].astype(jnp.float32)]
    psum x1 -> x0, waiting for transfers between devices: 60.7 us -> none  [on_device(): probe_grad = lax.psum(probe_sum, 'obj') / math.sqrt(slot_total)]
  transfers between devices with their start and end apart: 7 -> 0, of which waited for: 6 -> 0; matrix products, arithmetic and copies ran while one was open for 2% -> 0% of each run, Pallas kernels for 0% -> 0%
where the time goes in v1:
time: 135 us; the launch traced here: 134 us
  Pallas kernels  127 us (94%)
  local copies, waits for them, and re-layouts  6.65 us (5%)
    pallas_call x1, Pallas kernels, on_device(): pl.pallas_call(kernel, out_shape=(jax.ShapeDtypeStruct((2, 512, 512), F32...  127 us
    unnamed x6, local copies, waits for them, and re-layouts  5.45 us

profile of v1, /device:TPU:1, one launch (start us, length us, event | category | flops | bytes accessed | tf_op | source)
XLA Modules:
  0.0 133.9 jit_solution(16279906661664300518)
XLA Ops:
  0.6 0.8 copy.11
  1.4 0.6 reshape.10.row_ref
  2.0 0.8 copy.12
  2.7 0.6 reshape.11.col_ref
  3.3 126.6 %shard_map.86 = (f32[2,512,512]{2,1,0:T(8,128)}, f32[2,256,256]{2,1,0:T(8,128)}) custom-call(s32[32]{0:T(128)} %reshape.10.row_ref, s32[32]{0:T(128)} %reshape.11.col_ref, f32[2,512,512]{2,1,0:T(8,128)} %obj.1, f32[2,256,256]{2,1,0:T(8,128)} %probe.1, bf16[32,256,256]{2,1,0:T(8,128)(2,1)} %bitcast.3, bf16[512,512]{1,0:T(8,128)(2,1)} %constant.4.clone.ltab, ...), custom_call_target="tpu_custom_call" | custom-call | flops 17179869184 | bytes 10485760 | tf_op jit(solution)/shard_map/pallas_call | solution.py:526
  130.0 0.0 copy-start
  130.0 3.1 %copy.15 = f32[2,512,512]{2,1,0:T(8,128)} copy(f32[2,512,512]{2,1,0:T(8,128)} %get-tuple-element.8) | data formatting | bytes 4194304
  133.1 0.0 copy-done
  133.1 0.8 copy.16
Async XLA Ops:
  130.0 3.1 %copy-start = (f32[2,256,256]{2,1,0:T(8,128)S(1)}, f32[2,256,256]{2,1,0:T(8,128)}, u32[]{:S(2)}) copy-start(f32[2,256,256]{2,1,0:T(8,128)} %get-tuple-element.5) | copy-start | bytes 1572868

commit v2 on v1

v2 whole, which is shorter than its diff:
```python
import functools
import math

import jax
import jax.numpy as jnp
import ml_dtypes
import numpy as np
from jax import lax
from jax.experimental import pallas as pl
from jax.experimental.pallas import tpu as pltpu
from jax.sharding import PartitionSpec as P

MESH = pl.DeviceIdType.MESH
F32 = jnp.float32
BF16 = jnp.bfloat16

ORDER = [
    (0, 0), (1, 1), (3, 1), (1, 0), (3, 0), (0, 1), (2, 1), (1, 3),
    (3, 3), (1, 2), (3, 2), (0, 3), (2, 3), (2, 2), (0, 2), (2, 0),
]
CODES = [dz * 4 + dx for dz, dx in ORDER]
GROUPS = [(1, 4), (4, 8), (8, 12), (12, 14), (14, 16)]
RP = 32
CH = 32
EC = 32
PLAN = [
    ("X", 0), ("H", 0), ("X", 1), ("F", 0), ("H", 1), ("X", 2), ("F", 1), ("H", 2), ("X", 3), ("F", 2),
    ("H", 3), ("F", 3), ("A", 0), ("A", 1), ("A", 2), ("A", 3), ("D", 0), ("B", 0), ("D", 1), ("B", 1),
    ("D", 2), ("N", 0), ("B", 2), ("D", 3), ("N", 1), ("T", 0), ("B", 3), ("T", 1), ("N", 2), ("T", 2),
    ("N", 3), ("T", 3),
]


def dft_tables(length):
    grid = np.arange(length)
    angle = 2.0 * math.pi / length * (grid[:, None] * grid[None, :] % length)
    real = np.cos(angle) / math.sqrt(length)
    imag = -np.sin(angle) / math.sqrt(length)
    left = np.block([[real, -imag], [imag, real]])
    right = np.block([[real, imag], [-imag, real]])
    return left.astype(ml_dtypes.bfloat16), right.astype(ml_dtypes.bfloat16)


def code_of(n):
    return functools.reduce(lambda a, t: jnp.where(n == t, CODES[t], a), range(1, 16), jnp.int32(0))


def kernel(
    row_ref, col_ref, obj, probe, amps, ltab, rtab,
    out, rim_r, lrim_r, g_r,
    amp, ext, grad, term, patch, ebuf, hbuf, dbuf, bbuf, wide, pacc,
    strip_s, strip_r, low_s, low_r, corner_r,
    sib_s, sib_r, kept, y_s, y_r, q_s, q_r, x_s, x_r, g_s,
    rim_s, lrim_s, crim_r,
    local_sem, halo_ss, halo_rs, amp_ss, amp_rs, sib_ss, sib_rs, y_ss, y_rs, q_ss, q_rs, x_ss, x_rs, g_ss, g_rs, rim_ss, rim_rs,
):
    me = lax.axis_index("scan")
    band = lax.axis_index("obj")
    z, x = me // 4, me % 4
    yy, core = band // 2, band % 2
    left, right = (me + 15) % 16, (me + 1) % 16
    above, below = (band + 7) % 8, (band + 1) % 8

    barrier = pltpu.get_barrier_semaphore()
    for d in range(1, 16):
        pl.semaphore_signal(barrier, inc=1, device_id={"scan": (me + d) % 16}, device_id_type=MESH)
    for d in range(1, 8):
        pl.semaphore_signal(barrier, inc=1, device_id={"obj": (band + d) % 8}, device_id_type=MESH)

    def remote(src, dst, ss, rs, where):
        return pltpu.make_async_remote_copy(
            src_ref=src, dst_ref=dst, send_sem=ss, recv_sem=rs, device_id=where, device_id_type=MESH
        )

    tile_in = []
    for p in range(2):
        for b in range(4):
            cp = pltpu.make_async_copy(
                obj.at[p, :, pl.ds(b * 128, 128)], ext.at[p, b, pl.ds(0, 512)], local_sem.at[p * 4 + b]
            )
            cp.start()
            tile_in.append(cp)
    own_in = []
    for s in range(2):
        cp = pltpu.make_async_copy(amps.at[2 * me + s], amp.at[s * 16], local_sem.at[8 + s])
        cp.start()
        own_in.append(cp)
    pl.semaphore_wait(barrier, 22)

    def amp_copy(t, s):
        dz, dx = ORDER[t]
        target = ((z + dz) % 4) * 4 + (x + dx) % 4
        at = s * 16 + CODES[t]
        return remote(amps.at[2 * target + s], amp.at[at], amp_ss.at[at], amp_rs.at[at], {"scan": target})

    sends = [(t, s) for g, e in GROUPS for s in range(2) for t in range(g, e)]
    for t, s in sends[:6]:
        amp_copy(t, s).start()
    for cp in tile_in:
        cp.wait()

    def round_rows(i, c):
        rows = pl.ds(pl.multiple_of(i * 64, 64), 64)
        for p in range(2):
            for b in range(4):
                v = ext[p, b, rows, :].astype(BF16)
                ext[p, b, rows, :] = v.astype(F32)
                if b < 2:
                    strip_s[i // 4, p, b, pl.ds(pl.multiple_of(i % 4 * 64, 64), 64), :] = v
        return c

    lax.fori_loop(0, 8, round_rows, 0)

    def low_rows(i, c):
        rows = pl.ds(pl.multiple_of(i * 64, 64), 64)
        for p in range(2):
            for b in range(4):
                low_s[p, b, rows, :] = ext[p, b, rows, :].astype(BF16)
        return c

    lax.fori_loop(0, 4, low_rows, 0)

    strip_cps = [
        remote(strip_s.at[h], strip_r.at[h], halo_ss.at[3 * h], halo_rs.at[3 * h], {"scan": left}) for h in range(2)
    ]
    for cp in strip_cps:
        cp.start()
    low_cp = remote(low_s, low_r, halo_ss.at[1], halo_rs.at[1], {"obj": above})
    low_cp.start()

    for t, s in sends[6:]:
        amp_copy(t, s).start()

    def zero_rows(i, c):
        rows = pl.ds(pl.multiple_of(i * 64, 64), 64)
        nil = jnp.zeros((64, 128), F32)
        for p in range(2):
            for b in range(3):
                ext[p, 6 + b, rows, :] = nil
            for b in range(6):
                grad[p, b, rows, :] = nil
        return c

    lax.fori_loop(0, 12, zero_rows, 0)

    def zero_terms(i, c):
        nil = jnp.zeros((RP, 128), F32)
        term[i, 0:RP, :] = nil
        term[i, RP + 256 : RP + 256 + RP, :] = nil
        return c

    lax.fori_loop(0, 24, zero_terms, 0)
    term[24] = jnp.zeros((256 + 2 * RP, 128), F32)

    strip_cps[0].wait_recv()
    corner_cp = remote(strip_r.at[0], corner_r, halo_ss.at[2], halo_rs.at[2], {"obj": above})
    corner_cp.start()

    def strip_rows(h):
        def rows_of(i, c):
            rows = pl.ds(pl.multiple_of(i * 64, 64), 64)
            dest = pl.ds(pl.multiple_of(h * 256 + i * 64, 64), 64)
            for p in range(2):
                for b in range(2):
                    ext[p, 4 + b, dest, :] = strip_r[h, p, b, rows, :].astype(F32)
            return c

        lax.fori_loop(0, 4, rows_of, 0)

    strip_rows(0)
    low_cp.wait_recv()

    def low_in(i, c):
        rows = pl.ds(pl.multiple_of(i * 64, 64), 64)
        dest = pl.ds(pl.multiple_of(512 + i * 64, 64), 64)
        for p in range(2):
            for b in range(4):
                ext[p, b, dest, :] = low_r[p, b, rows, :].astype(F32)
        return c

    lax.fori_loop(0, 4, low_in, 0)
    strip_cps[1].wait_recv()
    strip_rows(1)
    corner_cp.wait_recv()

    def corner_in(i, c):
        rows = pl.ds(pl.multiple_of(i * 64, 64), 64)
        dest = pl.ds(pl.multiple_of(512 + i * 64, 64), 64)
        for p in range(2):
            for b in range(2):
                ext[p, 4 + b, dest, :] = corner_r[p, b, rows, :].astype(F32)
        return c

    lax.fori_loop(0, 4, corner_in, 0)
    for cp in own_in:
        cp.wait()

    lane = lax.broadcasted_iota(jnp.int32, (EC, 128), 1)

    def owner_of(n):
        code = code_of(n)
        dz, dx = code // 4, code % 4
        return code, ((z + 4 - dz) % 4) * 4 + (x + 4 - dx) % 4

    def amp_wait(at):
        pltpu.make_async_remote_copy(
            src_ref=amp.at[at], dst_ref=amp.at[at], send_sem=amp_ss.at[at], recv_sem=amp_rs.at[at],
            device_id={"scan": right}, device_id_type=MESH,
        ).wait_recv()

    def four(v):
        slots = []
        for a in range(2):
            code, owner = owner_of(2 * v + a)
            for s in range(2):
                at = s * 16 + code
                row = row_ref[s, owner]
                col = col_ref[s, owner]
                c0 = jnp.maximum(col, 0)
                slots.append((at, jnp.maximum(row, 0), jnp.where(row >= 0, c0 // 128, 6), c0 % 128))

        def arrived(k):
            if k < 2:
                pl.when(v > 0)(functools.partial(amp_wait, slots[k][0]))
            else:
                amp_wait(slots[k][0])

        def exit_wave(k):
            at, r0, block, shift = slots[k]
            for rc in range(0, 256, EC):
                rows = slice(rc, rc + EC)
                f = []
                for p in range(2):
                    raw = [ext[p, block + q, pl.ds(r0 + rc, EC), :] for q in range(3)]
                    f.append([
                        pltpu.roll(jnp.where(lane >= shift, raw[b], raw[b + 1]).astype(BF16), (128 - shift) % 128, 1)
                        for b in range(2)
                    ])
                for b in range(2):
                    lanes = slice(b * 128, b * 128 + 128)
                    fr, fi = f[0][b].astype(F32), f[1][b].astype(F32)
                    pr, pi = probe[0, rows, lanes], probe[1, rows, lanes]
                    patch[k, 0, rows, lanes] = f[0][b]
                    patch[k, 1, rows, lanes] = f[1][b]
                    ebuf[k, rows, lanes] = (pr * fr - pi * fi).astype(BF16)
                    ebuf[k, 256 + rc : 256 + rc + EC, lanes] = (pr * fi + pi * fr).astype(BF16)

        def half_to(k):
            h = jnp.dot(ltab[...], ebuf[k], preferred_element_type=F32).astype(BF16)
            hbuf[k, :, 0:256] = h[0:256]
            hbuf[k, :, 256:512] = h[256:512]

        def far_to(k):
            wide[k] = jnp.dot(hbuf[k], rtab[...], preferred_element_type=F32)

        def differ(k):
            at = slots[k][0]
            for rc in range(0, 256, EC):
                rows = slice(rc, rc + EC)
                fr, fi = wide[k, rows, 0:256], wide[k, rows, 256:512]
                m = amp[at, rows, :].astype(F32)
                scale = m * lax.rsqrt(jnp.maximum(fr * fr + fi * fi, 0.01)) - 1.0
                dbuf[k, rows, :] = (fr * scale).astype(BF16)
                dbuf[k, 256 + rc : 256 + rc + EC, :] = (fi * scale).astype(BF16)

        def back_to(k):
            h = jnp.dot(rtab[...], dbuf[k], preferred_element_type=F32).astype(BF16)
            bbuf[k, :, 0:256] = h[0:256]
            bbuf[k, :, 256:512] = h[256:512]

        def near_to(k):
            wide[4 + k] = jnp.dot(bbuf[k], ltab[...], preferred_element_type=F32)

        def terms(k):
            at, r0, block, shift = slots[k]
            n, second = k // 2, k % 2 == 1
            for rc in range(0, 256, EC):
                rows = slice(rc, rc + EC)
                trail = [None, None]
                for b in range(2):
                    lanes = slice(b * 128, b * 128 + 128)
                    nr = wide[4 + k, rows, b * 128 : b * 128 + 128]
                    ni = wide[4 + k, rows, 256 + b * 128 : 256 + b * 128 + 128]
                    pr, pi = probe[0, rows, lanes], probe[1, rows, lanes]
                    fr, fi = patch[k, 0, rows, lanes].astype(F32), patch[k, 1, rows, lanes].astype(F32)
                    tt = (pr * nr + pi * ni, pr * ni - pi * nr)
                    for p in range(2):
                        turned = pltpu.roll(tt[p].astype(BF16), shift, 1).astype(F32)
                        before = trail[p] if b else jnp.zeros_like(turned)
                        term[k * 6 + p * 3 + b, RP + rc : RP + rc + EC, :] = jnp.where(lane >= shift, turned, before)
                        trail[p] = turned
                    pt = (fr * nr + fi * ni, fr * ni - fi * nr)
                    for p in range(2):
                        pacc[n, p, rows, lanes] = pacc[n, p, rows, lanes] + pt[p] if second else pt[p]
                for p in range(2):
                    term[k * 6 + p * 3 + 2, RP + rc : RP + rc + EC, :] = jnp.where(
                        lane >= shift, jnp.zeros_like(trail[p]), trail[p]
                    )

        stages = {"A": arrived, "X": exit_wave, "H": half_to, "F": far_to, "D": differ, "B": back_to, "N": near_to, "T": terms}
        for stage, k in PLAN:
            stages[stage](k)

    def gather(v, blocks):
        places = []
        for w in range(4):
            code, owner = owner_of(2 * v + w // 2)
            row = jnp.maximum(row_ref[w % 2, owner], 0)
            block = jnp.maximum(col_ref[w % 2, owner], 0) // 128
            places.append((row, block))
        picks = [
            [
                [
                    jnp.where((b - block >= 0) & (b - block < 3), w * 6 + p * 3 + b - block, 24)
                    for w, (row, block) in enumerate(places)
                ]
                for b in range(6)
            ]
            for p in range(2)
        ]

        def rows_of(ic, c):
            rows = pl.ds(pl.multiple_of(ic * CH, CH), CH)
            starts = [jnp.clip(ic * CH - row, -RP, 256) + RP for row, block in places]
            for b in blocks:
                for p in range(2):
                    acc = grad[p, b, rows, :]
                    for w in range(4):
                        acc = acc + term[picks[p][b][w], pl.ds(starts[w], CH), :]
                    grad[p, b, rows, :] = acc
            return c

        lax.fori_loop(0, 768 // CH, rows_of, 0)

    def sib_copy(i):
        return remote(sib_s.at[i], sib_r.at[i], sib_ss.at[i], sib_rs.at[i], {"obj": 2 * yy + 1 - core})

    def y_copy(i, d):
        to = (yy + d) % 4
        return remote(
            y_s.at[i, to], y_r.at[i, d - 1], y_ss.at[i * 3 + d - 1], y_rs.at[i * 3 + d - 1], {"obj": 2 * to + core}
        )

    def q_copy(i, a):
        code, owner = owner_of(2 * i + a)
        return remote(q_s.at[i, a], q_r.at[code], q_ss.at[code], q_rs.at[code], {"scan": owner // 4 * 4 + x})

    mine = pl.ds(pl.multiple_of(core * 128, 128), 128)
    other = pl.ds(pl.multiple_of((1 - core) * 128, 128), 128)

    def sib_stage(i):
        for a in range(2):
            for p in range(2):
                sib_s[i, a, p] = pacc[a, p, other, :].astype(BF16)
                kept[i % 2, a, p] = pacc[a, p, mine, :]
        sib_copy(i).start()

    def y_stage(i):
        sib_copy(i).wait_recv()
        for a in range(2):
            for p in range(2):
                total = kept[i % 2, a, p] + sib_r[i, a, p].astype(F32)
                for q in range(4):
                    y_s[i, q, a, p] = total[q * 32 : q * 32 + 32].astype(BF16)
        for d in range(1, 4):
            y_copy(i, d).start()

    def q_stage(i):
        for d in range(1, 4):
            y_copy(i, d).wait_recv()
        for a in range(2):
            for p in range(2):
                total = y_s[i, yy, a, p].astype(F32)
                for d in range(3):
                    total = total + y_r[i, d, a, p].astype(F32)
                q_s[i, a, p] = total.astype(BF16)

        for a in range(2):
            code, owner = owner_of(2 * i + a)

            @pl.when(code >= 4)
            def _():
                q_copy(i, a).start()

            @pl.when(code < 4)
            def _():
                q_r[code] = q_s[i, a]

    def step(v, c):
        @pl.when(v >= 1)
        def _():
            y_stage(v - 1)

        @pl.when(v >= 2)
        def _():
            q_stage(v - 2)

        four(v)
        sib_stage(v)
        gather(v, (4, 5))

        @pl.when(v < 7)
        def _():
            gather(v, (0, 1, 2, 3))

        return c

    lax.fori_loop(0, 8, step, 0)

    def rim_low_half(i, c):
        rows = pl.ds(pl.multiple_of(i * 64, 64), 64)
        src = pl.ds(pl.multiple_of(256 + i * 64, 64), 64)
        for p in range(2):
            for b in range(2):
                rim_s[1, p, b, rows, :] = grad[p, 4 + b, src, :].astype(BF16)
        return c

    lax.fori_loop(0, 4, rim_low_half, 0)
    rim_b = remote(rim_s.at[1], rim_r.at[1], rim_ss.at[1], rim_rs.at[1], {"scan": right})
    rim_b.start()
    y_stage(7)

    def corner_out(i, c):
        rows = pl.ds(pl.multiple_of(i * 64, 64), 64)
        low = pl.ds(pl.multiple_of(512 + i * 64, 64), 64)
        for p in range(2):
            for b in range(2):
                lrim_s[0, p, b, rows, :] = grad[p, 4 + b, low, :].astype(BF16)
        return c

    lax.fori_loop(0, 4, corner_out, 0)
    crim_cp = remote(lrim_s.at[0], crim_r, rim_ss.at[0], rim_rs.at[0], {"obj": below})
    crim_cp.start()
    q_stage(6)
    gather(7, (0, 1, 2, 3))

    def low_out(i, c):
        rows = pl.ds(pl.multiple_of(i * 64, 64), 64)
        low = pl.ds(pl.multiple_of(512 + i * 64, 64), 64)
        for p in range(2):
            for b in range(4):
                lrim_s[1 + b // 2, p, b % 2, rows, :] = grad[p, b, low, :].astype(BF16)
        return c

    lax.fori_loop(0, 4, low_out, 0)
    lrim_cp = remote(lrim_s.at[pl.ds(1, 2)], lrim_r, rim_ss.at[2], rim_rs.at[2], {"obj": below})
    lrim_cp.start()
    out_cps = []
    for p in range(2):
        for b in range(4):
            cp = pltpu.make_async_copy(
                grad.at[p, b, pl.ds(0, 512)], out.at[p, :, pl.ds(b * 128, 128)], local_sem.at[p * 4 + b]
            )
            cp.start()
            out_cps.append(cp)
    crim_cp.wait_recv()

    def rim_top_half(i, c):
        rows = pl.ds(pl.multiple_of(i * 64, 64), 64)
        for p in range(2):
            for b in range(2):
                rim_s[0, p, b, rows, :] = (grad[p, 4 + b, rows, :] + crim_r[p, b, rows, :].astype(F32)).astype(BF16)
        return c

    lax.fori_loop(0, 4, rim_top_half, 0)
    rim_t = remote(rim_s.at[0], rim_r.at[0], rim_ss.at[3], rim_rs.at[3], {"scan": right})
    rim_t.start()
    q_stage(7)

    for code in range(4, 16):
        remote(q_s.at[0, 0], q_r.at[code], q_ss.at[code], q_rs.at[code], {"scan": right}).wait_recv()

    def x_copy(dx):
        return remote(x_s.at[dx], x_r.at[dx], x_ss.at[dx], x_rs.at[dx], {"scan": z * 4 + (x + 4 - dx) % 4})

    for dx in (1, 3, 2, 0):
        for p in range(2):
            total = q_r[dx, p].astype(F32)
            for dz in range(1, 4):
                total = total + q_r[dz * 4 + dx, p].astype(F32)
            x_s[dx, p] = total.astype(BF16)
        if dx:
            x_copy(dx).start()
    for dx in range(1, 4):
        x_copy(dx).wait_recv()
    piece = core * 4 + yy
    for p in range(2):
        total = x_s[0, p].astype(F32)
        for dx in range(1, 4):
            total = total + x_r[dx, p].astype(F32)
        g_s[p] = (total * (1.0 / 16.0)).astype(BF16)

    def g_copy(d):
        return remote(g_s, g_r.at[piece], g_ss.at[d - 1], g_rs.at[d - 1], {"obj": (band + d) % 8})

    for d in range(1, 8):
        g_copy(d).start()
    own_g = pltpu.make_async_copy(g_s, g_r.at[piece], local_sem.at[8])
    own_g.start()
    for d in range(1, 8):
        frm = (band + 8 - d) % 8
        at = frm % 2 * 4 + frm // 2
        remote(g_s, g_r.at[at], g_ss.at[d - 1], g_rs.at[d - 1], {"obj": frm}).wait_recv()
    for cp in (lrim_cp, rim_b, rim_t):
        cp.wait_recv()

    for cp in (*strip_cps, low_cp, corner_cp, crim_cp, rim_b, lrim_cp, rim_t):
        cp.wait_send()
    for t, s in sends:
        amp_copy(t, s).wait_send()

    def drain(i, c):
        sib_copy(i).wait_send()
        for d in range(1, 4):
            y_copy(i, d).wait_send()

        for a in range(2):

            @pl.when(owner_of(2 * i + a)[0] >= 4)
            def _():
                q_copy(i, a).wait_send()
        return c

    lax.fori_loop(0, 8, drain, 0)
    for d in range(1, 8):
        g_copy(d).wait_send()
    for dx in range(1, 4):
        x_copy(dx).wait_send()
    own_g.wait()
    for cp in out_cps:
        cp.wait()


def finish_kernel(main, rim, low, pieces, out, pout):
    out[...] = main[...]
    for b in range(2):
        for h in range(2):
            at = (0, slice(h * 256, h * 256 + 256), slice(b * 128, b * 128 + 128))
            out[at] = out[at] + rim[h, 0, b].astype(F32)
    for b in range(4):
        at = (0, slice(0, 256), slice(b * 128, b * 128 + 128))
        out[at] = out[at] + low[b // 2, 0, b % 2].astype(F32)
    for q in range(8):
        pout[0, 0, q * 32 : q * 32 + 32, :] = pieces[q, 0].astype(F32)


def on_device(object_field, probe, amplitudes, corner_row, corner_col):
    ltab, rtab = dft_tables(256)
    vm = pltpu.VMEM
    dma = pltpu.SemaphoreType.DMA
    anywhere = pl.BlockSpec(memory_space=pl.ANY)
    inside = pl.BlockSpec(memory_space=pltpu.VMEM)
    scalar = pl.BlockSpec(memory_space=pltpu.SMEM)
    main, rim, low, pieces = pl.pallas_call(
        kernel,
        out_shape=(
            jax.ShapeDtypeStruct((2, 512, 512), F32),
            jax.ShapeDtypeStruct((2, 2, 2, 256, 128), BF16),
            jax.ShapeDtypeStruct((2, 2, 2, 256, 128), BF16),
            jax.ShapeDtypeStruct((8, 2, 32, 256), BF16),
        ),
        in_specs=[scalar, scalar, anywhere, inside, anywhere, inside, inside],
        out_specs=(anywhere,) * 4,
        scratch_shapes=[
            vm((32, 256, 256), BF16),
            vm((2, 9, 768, 128), F32),
            vm((2, 6, 768, 128), F32),
            vm((25, 256 + 2 * RP, 128), F32),
            vm((4, 2, 256, 256), BF16),
            vm((4, 512, 256), BF16),
            vm((4, 256, 512), BF16),
            vm((4, 512, 256), BF16),
            vm((4, 256, 512), BF16),
            vm((8, 256, 512), F32),
            vm((2, 2, 256, 256), F32),
            vm((2, 2, 2, 256, 128), BF16),
            vm((2, 2, 2, 256, 128), BF16),
            vm((2, 4, 256, 128), BF16),
            vm((2, 4, 256, 128), BF16),
            vm((2, 2, 256, 128), BF16),
            vm((8, 2, 2, 128, 256), BF16),
            vm((8, 2, 2, 128, 256), BF16),
            vm((2, 2, 2, 128, 256), F32),
            vm((8, 4, 2, 2, 32, 256), BF16),
            vm((8, 3, 2, 2, 32, 256), BF16),
            vm((8, 2, 2, 32, 256), BF16),
            vm((16, 2, 32, 256), BF16),
            vm((4, 2, 32, 256), BF16),
            vm((4, 2, 32, 256), BF16),
            vm((2, 32, 256), BF16),
            vm((2, 2, 2, 256, 128), BF16),
            vm((3, 2, 2, 256, 128), BF16),
            vm((2, 2, 256, 128), BF16),
            dma((10,)),
            dma((4,)), dma((4,)),
            dma((32,)), dma((32,)),
            dma((8,)), dma((8,)),
            dma((24,)), dma((24,)),
            dma((16,)), dma((16,)),
            dma((4,)), dma((4,)),
            dma((7,)), dma((7,)),
            dma((4,)), dma((4,)),
        ],
        compiler_params=pltpu.CompilerParams(
            collective_id=0, has_side_effects=True, vmem_limit_bytes=62 * 2**20
        ),
        cost_estimate=pl.CostEstimate(flops=32 * 16 * 2 * 256**3, bytes_accessed=10 * 2**20, transcendentals=32 * 65536),
    )(
        corner_row[0].T, corner_col[0].T, object_field, probe, amplitudes[0],
        jnp.asarray(ltab), jnp.asarray(rtab),
    )
    return tuple(
        pl.pallas_call(
            finish_kernel,
            grid=(2,),
            in_specs=[
                pl.BlockSpec((1, 512, 512), lambda p: (p, 0, 0)),
                pl.BlockSpec((2, 1, 2, 256, 128), lambda p: (0, p, 0, 0, 0)),
                pl.BlockSpec((2, 1, 2, 256, 128), lambda p: (0, p, 0, 0, 0)),
                pl.BlockSpec((8, 1, 32, 256), lambda p: (0, p, 0, 0)),
            ],
            out_specs=(
                pl.BlockSpec((1, 512, 512), lambda p: (p, 0, 0)),
                pl.BlockSpec((1, 1, 256, 256), lambda p: (0, p, 0, 0)),
            ),
            out_shape=(
                jax.ShapeDtypeStruct((2, 512, 512), F32),
                jax.ShapeDtypeStruct((1, 2, 256, 256), F32),
            ),
            compiler_params=pltpu.CompilerParams(vmem_limit_bytes=60 * 2**20),
        )(main, rim, low, pieces)
    )


def solution(mesh):
    return jax.shard_map(
        on_device,
        mesh=mesh,
        in_specs=(
            P(None, "obj", "scan"),
            P(),
            P("obj", "scan", None, None),
            P("obj", "scan", None),
            P("obj", "scan", None),
        ),
        out_specs=(P(None, "obj", "scan"), P("scan", None, None, None)),
        check_vma=False,
    )
```

time: 135 us -> 110 us (0.81)
  Pallas kernels: 127 us -> 110 us
  local copies, waits for them, and re-layouts: 6.65 us -> 0 us
    pallas_call x1, Pallas kernels: 127 us -> 106 us  [on_device(): pl.pallas_call(kernel, out_shape=(jax.ShapeDtypeStruct((2, 512, 512), F32...]
    unnamed x6 -> x0, local copies, waits for them, and re-layouts: 5.45 us -> none
    pallas_call x0 -> x1, Pallas kernels: none -> 3.15 us  [on_device(): pl.pallas_call(finish_kernel, grid=(2,), in_specs=[pl.BlockSpec((1, 512,...]
where the time goes in v2:
time: 110 us
  Pallas kernels  110 us (100%)
    pallas_call x1, Pallas kernels, on_device(): pl.pallas_call(kernel, out_shape=(jax.ShapeDtypeStruct((2, 512, 512), F32...  106 us
    pallas_call x1, Pallas kernels, on_device(): pl.pallas_call(finish_kernel, grid=(2,), in_specs=[pl.BlockSpec((1, 512,...  3.15 us

profile of v2, /device:TPU:1, one launch (start us, length us, event | category | flops | bytes accessed | tf_op | source)
XLA Modules:
  0.0 110.2 jit_solution(11097803245727242990)
XLA Ops:
  0.6 106.4 %shard_map.86 = (f32[2,512,512]{2,1,0:T(8,128)}, bf16[2,2,2,256,128]{4,3,2,1,0:T(8,128)(2,1)}, bf16[2,2,2,256,128]{4,3,2,1,0:T(8,128)(2,1)}, bf16[8,2,32,256]{3,2,1,0:T(8,128)(2,1)}) custom-call(s32[2,16]{1,0:T(2,128)} %bitcast.8, s32[2,16]{1,0:T(2,128)} %bitcast.9, f32[2,512,512]{2,1,0:T(8,128)} %obj.1, f32[2,256,256]{2,1,0:T(8,128)} %probe.1, ...), custom_call_target="tpu_custom_call" | custom-call | flops 17179869184 | bytes 10485760 | tf_op jit(solution)/shard_map/pallas_call | solution.py:554
  107.1 3.1 %shard_map.87 = (f32[2,512,512]{2,1,0:T(8,128)}, f32[1,2,256,256]{3,2,1,0:T(8,128)}) custom-call(f32[2,512,512]{2,1,0:T(8,128)} %get-tuple-element.6.main, bf16[2,2,2,256,128]{4,3,2,1,0:T(8,128)(2,1)} %get-tuple-element.7.rim, bf16[2,2,2,256,128]{4,3,2,1,0:T(8,128)(2,1)} %get-tuple-element.8.low, bf16[8,2,32,256]{3,2,1,0:T(8,128)(2,1)} %get-tuple-element.9.pieces), custom_call_target="tpu_custom_call" | custom-call | tf_op jit(solution)/shard_map/pallas_call | solution.py:613

commit v3 on v2

--- a/solution.py
+++ b/solution.py
@@ -19,7 +19,7 @@
     (3, 3), (1, 2), (3, 2), (0, 3), (2, 3), (2, 2), (0, 2), (2, 0),
 ]
 CODES = [dz * 4 + dx for dz, dx in ORDER]
-GROUPS = [(1, 4), (4, 8), (8, 12), (12, 14), (14, 16)]
+GROUPS = [(1, 2), (2, 4), (4, 6), (6, 8), (8, 10), (10, 12), (12, 14), (14, 16)]
 RP = 32
 CH = 32
 EC = 32

time: 110 us -> 109 us (level)
  Pallas kernels: 110 us -> 108 us
    pallas_call x1, Pallas kernels: 106 us -> 105 us  [on_device(): pl.pallas_call(kernel, out_shape=(jax.ShapeDtypeStruct((2, 512, 512), F32...]
where the time goes in v3:
time: 109 us
  Pallas kernels  108 us (99%)
    pallas_call x1, Pallas kernels, on_device(): pl.pallas_call(kernel, out_shape=(jax.ShapeDtypeStruct((2, 512, 512), F32...  105 us
    pallas_call x1, Pallas kernels, on_device(): pl.pallas_call(finish_kernel, grid=(2,), in_specs=[pl.BlockSpec((1, 512,...  3.15 us

profile of v3, /device:TPU:1, one launch (start us, length us, event | category | flops | bytes accessed | tf_op | source)
XLA Modules:
  0.0 108.5 jit_solution(8691283577414716193)
XLA Ops:
  0.6 104.8 %shard_map.86 = (f32[2,512,512]{2,1,0:T(8,128)}, bf16[2,2,2,256,128]{4,3,2,1,0:T(8,128)(2,1)}, bf16[2,2,2,256,128]{4,3,2,1,0:T(8,128)(2,1)}, bf16[8,2,32,256]{3,2,1,0:T(8,128)(2,1)}) custom-call(s32[2,16]{1,0:T(2,128)} %bitcast.8, s32[2,16]{1,0:T(2,128)} %bitcast.9, f32[2,512,512]{2,1,0:T(8,128)} %obj.1, f32[2,256,256]{2,1,0:T(8,128)} %probe.1, ...), custom_call_target="tpu_custom_call" | custom-call | flops 17179869184 | bytes 10485760 | tf_op jit(solution)/shard_map/pallas_call | solution.py:554
  105.4 3.1 %shard_map.87 = (f32[2,512,512]{2,1,0:T(8,128)}, f32[1,2,256,256]{3,2,1,0:T(8,128)}) custom-call(f32[2,512,512]{2,1,0:T(8,128)} %get-tuple-element.6.main, bf16[2,2,2,256,128]{4,3,2,1,0:T(8,128)(2,1)} %get-tuple-element.7.rim, bf16[2,2,2,256,128]{4,3,2,1,0:T(8,128)(2,1)} %get-tuple-element.8.low, bf16[8,2,32,256]{3,2,1,0:T(8,128)(2,1)} %get-tuple-element.9.pieces), custom_call_target="tpu_custom_call" | custom-call | tf_op jit(solution)/shard_map/pallas_call | solution.py:613

commit v4 on v3

--- a/solution.py
+++ b/solution.py
@@ -407,6 +407,24 @@
 
     lax.fori_loop(0, 8, step, 0)
 
+    def z_wait(code):
+        remote(q_s.at[0, 0], q_r.at[code], q_ss.at[code], q_rs.at[code], {"scan": right}).wait_recv()
+
+    def x_copy(dx):
+        return remote(x_s.at[dx], x_r.at[dx], x_ss.at[dx], x_rs.at[dx], {"scan": z * 4 + (x + 4 - dx) % 4})
+
+    def x_stage(dx):
+        for dz in range(1, 4):
+            z_wait(dz * 4 + dx)
+        for p in range(2):
+            total = q_r[dx, p].astype(F32)
+            for dz in range(1, 4):
+                total = total + q_r[dz * 4 + dx, p].astype(F32)
+            x_s[dx, p] = total.astype(BF16)
+        x_copy(dx).start()
+
+    x_stage(1)
+
     def rim_low_half(i, c):
         rows = pl.ds(pl.multiple_of(i * 64, 64), 64)
         src = pl.ds(pl.multiple_of(256 + i * 64, 64), 64)
@@ -467,25 +485,17 @@
     rim_t.start()
     q_stage(7)
 
-    for code in range(4, 16):
-        remote(q_s.at[0, 0], q_r.at[code], q_ss.at[code], q_rs.at[code], {"scan": right}).wait_recv()
-
-    def x_copy(dx):
-        return remote(x_s.at[dx], x_r.at[dx], x_ss.at[dx], x_rs.at[dx], {"scan": z * 4 + (x + 4 - dx) % 4})
-
-    for dx in (1, 3, 2, 0):
-        for p in range(2):
-            total = q_r[dx, p].astype(F32)
-            for dz in range(1, 4):
-                total = total + q_r[dz * 4 + dx, p].astype(F32)
-            x_s[dx, p] = total.astype(BF16)
-        if dx:
-            x_copy(dx).start()
+    x_stage(3)
+    x_stage(2)
+    for dz in range(1, 4):
+        z_wait(dz * 4)
     for dx in range(1, 4):
         x_copy(dx).wait_recv()
     piece = core * 4 + yy
     for p in range(2):
-        total = x_s[0, p].astype(F32)
+        total = q_r[0, p].astype(F32)
+        for dz in range(1, 4):
+            total = total + q_r[dz * 4, p].astype(F32)
         for dx in range(1, 4):
             total = total + x_r[dx, p].astype(F32)
         g_s[p] = (total * (1.0 / 16.0)).astype(BF16)

time: 109 us -> 109 us (level)
  no operation moved by 1% of the time
where the time goes in v4:
time: 109 us; the launch traced here: 108 us
  Pallas kernels  108 us (99%)
    pallas_call x1, Pallas kernels, on_device(): pl.pallas_call(kernel, out_shape=(jax.ShapeDtypeStruct((2, 512, 512), F32...  105 us
    pallas_call x1, Pallas kernels, on_device(): pl.pallas_call(finish_kernel, grid=(2,), in_specs=[pl.BlockSpec((1, 512,...  3.15 us

profile of v4, /device:TPU:1, one launch (start us, length us, event | category | flops | bytes accessed | tf_op | source)
XLA Modules:
  0.0 108.5 jit_solution(5714132884978823232)
XLA Ops:
  0.6 104.7 %shard_map.86 = (f32[2,512,512]{2,1,0:T(8,128)}, bf16[2,2,2,256,128]{4,3,2,1,0:T(8,128)(2,1)}, bf16[2,2,2,256,128]{4,3,2,1,0:T(8,128)(2,1)}, bf16[8,2,32,256]{3,2,1,0:T(8,128)(2,1)}) custom-call(s32[2,16]{1,0:T(2,128)} %bitcast.8, s32[2,16]{1,0:T(2,128)} %bitcast.9, f32[2,512,512]{2,1,0:T(8,128)} %obj.1, f32[2,256,256]{2,1,0:T(8,128)} %probe.1, ...), custom_call_target="tpu_custom_call" | custom-call | flops 17179869184 | bytes 10485760 | tf_op jit(solution)/shard_map/pallas_call | solution.py:564
  105.3 3.1 %shard_map.87 = (f32[2,512,512]{2,1,0:T(8,128)}, f32[1,2,256,256]{3,2,1,0:T(8,128)}) custom-call(f32[2,512,512]{2,1,0:T(8,128)} %get-tuple-element.6.main, bf16[2,2,2,256,128]{4,3,2,1,0:T(8,128)(2,1)} %get-tuple-element.7.rim, bf16[2,2,2,256,128]{4,3,2,1,0:T(8,128)(2,1)} %get-tuple-element.8.low, bf16[8,2,32,256]{3,2,1,0:T(8,128)(2,1)} %get-tuple-element.9.pieces), custom_call_target="tpu_custom_call" | custom-call | tf_op jit(solution)/shard_map/pallas_call | solution.py:623
